TPU v7x, 32 devices: a whole 2x2x4 slice. The times are simulated.
32 devices in a mesh: dp: 8 (over z, x), tensor: 4 (over y, core).
Axes of the slice: x: 2, y: 2, z: 4, core: 2. Of those that a mesh axis runs over, the one named last changes fastest.
Arguments:
- inputs: bfloat16 [4, 512, 4096], P(None, ('dp', 'tensor')), may hold values from -6 to 6
- membrane: float32 [4, 512, 14336], P(None, 'dp', 'tensor'), may hold values from -6 to 6
- spike_grad: bfloat16 [4, 512, 14336], P(None, 'dp', 'tensor'), may hold values from -6 to 6
- decay: float32 [14336], P('tensor'), may hold values from 0.2 to 0.9
- gate_weight: bfloat16 [4096, 14336], P('dp', 'tensor'), may hold values from -0.09375 to 0.09375
Outputs:
- input_grad: bfloat16 [4, 512, 4096], P(None, ('dp', 'tensor'))
- weight_grad: bfloat16 [4096, 14336], P('dp', 'tensor')
All inputs are finite; a program needn't handle non-finite values.
Results may differ from a plain program's by a relative error of at most 0.022.
Values may be sent and summed in bfloat16 or wider, within the bound.
A program may use at most 192 MiB of HBM per device.

v0:
```python
import jax
import jax.numpy as jnp
from jax import lax
from jax.sharding import PartitionSpec as P

surrogate_slope = 2.0
fire_level = 0.5


def unit_gradients(membrane, spike_grad, decay):
    scaled = surrogate_slope * (membrane - fire_level)
    logistic = jax.nn.sigmoid(scaled)
    surrogate = surrogate_slope * logistic * (1.0 - logistic)
    local_terms = spike_grad.astype(jnp.float32) * surrogate
    carried = jnp.zeros_like(local_terms[0])
    results = []
    for step in reversed(range(local_terms.shape[0])):
        carried = local_terms[step] + decay * carried
        results.append(carried)
    return jnp.stack(results[::-1]).astype(jnp.bfloat16)


def body(inputs, membrane, spike_grad, decay, gate_weight):
    gathered = lax.all_gather(inputs, "tensor", axis=1, tiled=True)
    unit_grad = unit_gradients(membrane, spike_grad, decay)
    steps_count, token_count, hidden_local = unit_grad.shape
    feature_count = gathered.shape[2]
    flat_grads = unit_grad.reshape(steps_count * token_count, hidden_local)
    input_terms = lax.dot_general(
        flat_grads,
        lax.all_gather(gate_weight, "dp", axis=0, tiled=True),
        (((1,), (1,)), ((), ())),
        preferred_element_type=jnp.float32,
    )
    input_terms = input_terms.reshape(steps_count, token_count, feature_count)
    input_total = lax.psum_scatter(
        input_terms.astype(jnp.bfloat16), "tensor", scatter_dimension=1, tiled=True
    )
    dp_count = lax.axis_size("dp")
    rows_local = feature_count // dp_count
    local_term = jnp.einsum(
        "sti,stf->if", gathered, unit_grad, preferred_element_type=jnp.float32
    ).astype(jnp.bfloat16)
    row_blocks = local_term.reshape(dp_count, rows_local, hidden_local)
    arrived = lax.all_to_all(row_blocks, "dp", split_axis=0, concat_axis=0, tiled=True)
    total_sum = jnp.sum(arrived, axis=0, dtype=jnp.float32)
    weight_grad = (total_sum / dp_count).astype(jnp.bfloat16)
    return (input_total, weight_grad)


def solution(mesh):
    return jax.shard_map(
        body,
        mesh=mesh,
        in_specs=(
            P(None, ("dp", "tensor"), None),
            P(None, "dp", "tensor"),
            P(None, "dp", "tensor"),
            P("tensor"),
            P("dp", "tensor"),
        ),
        out_specs=(P(None, ("dp", "tensor"), None), P("dp", "tensor")),
        check_vma=False,
    )
```

profile of v0, /device:TPU:0, one launch (start us, length us, event | category | flops | bytes accessed | tf_op | source)
XLA Modules:
  0.0 1074.0 jit_solution(16243453344141025685)
XLA Ops:
  7.2 0.0 copy-start.1
  7.2 0.0 copy-start
  7.2 0.0 all-gather.5.cloned.1.call-start
  7.2 0.7 all-gather.5.cloned.1.call-update
  7.9 0.0 all-gather.3.cloned.1.call-start
  8.0 0.7 all-gather.3.cloned.1.call-update
  8.7 0.0 copy-done.1
  8.7 0.0 copy-done
  8.7 3.4 multiply_multiply_fusion
  12.1 0.3 fusion.5
  12.3 0.1 fusion.7
  12.5 22.4 %all-gather.5.cloned.1.call-done = bf16[4,64,4096]{2,1,0:T(8,128)(2,1)} async-done(((bf16[4,16,4096]{2,1,0:T(8,128)(2,1)}), bf16[4,64,4096]{2,1,0:T(8,128)(2,1)}) %all-gather.5.cloned.1.call-update) | async-done | bytes 2097168 | tf_op jit(solution)/shard_map/all_gather | solution.py:24
  34.9 14.2 %bitcast_convert_fusion = bf16[3584,4096]{1,0:T(8,128)(2,1)} fusion(bf16[4,64,4096]{2,1,0:T(8,128)(2,1)} %all-gather.5.cloned.1.call-done, bf16[1,64,3584]{2,1,0:T(8,128)(2,1)S(1)} %get-tuple-element.6, bf16[1,64,3584]{2,1,0:T(8,128)(2,1)S(1)} %get-tuple-element.8, bf16[1,64,3584]{2,1,0:T(8,128)(2,1)S(1)} %get-tuple-element.7, ...), kind=kOutput, calls=%fused_computation | convolution fusion | flops 7533625344 | bytes 33292288 | tf_op jit(solution)/shard_map/sti,stf->if/dot_general | solution.py:41
  49.1 20.2 %copy.13 = bf16[448,8,8,512]{3,2,0,1:T(8,128)(2,1)} copy(bf16[448,8,8,512]{3,2,1,0:T(8,128)(2,1)} %bitcast.14) | data formatting | bytes 58720256 | tf_op jit(solution)/shard_map/reshape | solution.py:44
  69.3 6.7 all-to-all-start
  76.0 0.0 reduce-scatter.2.cloned.1.call-start
  76.1 919.8 %all-gather.3.cloned.1.call-done = bf16[4096,3584]{1,0:T(8,128)(2,1)} async-done(((bf16[512,3584]{1,0:T(8,128)(2,1)}), bf16[4096,3584]{1,0:T(8,128)(2,1)}) %all-gather.3.cloned.1.call-update) | async-done | bytes 29360144 | tf_op jit(solution)/shard_map/all_gather | solution.py:31
  995.9 15.1 %fusion.2 = bf16[4,64,4096]{2,1,0:T(8,128)(2,1)} fusion(bf16[4096,3584]{1,0:T(8,128)(2,1)} %all-gather.3.cloned.1.call-done, bf16[1,64,3584]{2,1,0:T(8,128)(2,1)S(1)} %get-tuple-element.6, bf16[1,64,3584]{2,1,0:T(8,128)(2,1)S(1)} %get-tuple-element.8, bf16[1,64,3584]{2,1,0:T(8,128)(2,1)S(1)} %get-tuple-element.7, bf16[1,64,3584]{2,1,0:T(8,128)(2,1)S(1)} %get-tuple-element.4), kind=kOutput, calls=%fused_computation.6 | convolution fusion | flops 7519993856 | bytes 33292288 | tf_op jit(solution)/shard_map/dot_general | solution.py:29
  1010.9 0.0 reduce-scatter.2.cloned.1.call-update
  1011.0 0.0 all-to-all-done
  1011.0 13.4 %convert_reduce_fusion = f32[512,3584]{0,1:T(8,128)} fusion(bf16[8,512,3584]{1,2,0:T(8,128)(2,1)} %all-to-all-done), kind=kLoop, calls=%fused_computation.1 | loop fusion | flops 27525120 | bytes 36700160 | tf_op jit(solution)/shard_map/reduce_sum | solution.py:46
  1024.4 6.0 multiply_convert_fusion
  1030.4 5.9 copy.9
  1036.4 31.1 %reduce-scatter.2.cloned.1.call-done = bf16[4,16,4096]{2,1,0:T(8,128)(2,1)} async-done(((bf16[4,64,4096]{2,1,0:T(8,128)(2,1)}), bf16[4,16,4096]{2,1,0:T(8,128)(2,1)}) %reduce-scatter.2.cloned.1.call-update) | async-done | bytes 524304 | tf_op jit(solution)/shard_map/reduce_scatter | solution.py:36
  (1 shorter events, 0.0 us)
Async XLA Ops:
  7.2 1.5 copy-start.1
  7.2 1.5 copy-start
  7.2 27.7 %all-gather.5.cloned.1.call-start = ((), (), s32[]{:S(2)}) async-start(), calls=%async_computation.4 | async-start | bytes 2621440 | tf_op jit(solution)/shard_map/all_gather | solution.py:24
  7.9 987.9 %all-gather.3.cloned.1.call-start = ((), (), s32[]{:S(2)}) async-start(), calls=%async_computation.2 | async-start | bytes 33030144 | tf_op jit(solution)/shard_map/all_gather | solution.py:31
  69.3 941.7 %all-to-all-start = ((bf16[8,512,3584]{1,2,0:T(8,128)(2,1)}), bf16[8,512,3584]{1,2,0:T(8,128)(2,1)}, u32[]{:S(2)}, u32[]{:S(2)}) async-start(bf16[8,512,3584]{1,2,0:T(8,128)(2,1)} %bitcast.13), calls=%async_computation.1 | async-start | bytes 58720256 | tf_op jit(solution)/shard_map/all_to_all | solution.py:45
  76.0 991.5 %reduce-scatter.2.cloned.1.call-start = ((), (), s32[]{:S(2)}) async-start(), calls=%async_computation.3 | async-start | bytes 2621440 | tf_op jit(solution)/shard_map/reduce_scatter | solution.py:36
Sparse Core Ops, SparseCore 0:
  9.6 25.2 all-gather.4
  36.4 959.3 all-gather.2
  1011.1 56.3 reduce-scatter.1
where the time goes:
time: 1070 us
  waiting for transfers between devices  975 us (91%)
  matrix products  29.3 us (3%)
  local copies, waits for them, and re-layouts  26.1 us (2%)
  other arithmetic  23.2 us (2%)
  between operations  13.8 us (1%)
    all_gather x1, waiting for transfers between devices, body(): lax.all_gather(gate_weight, 'dp', axis=0, tiled=True)  920 us
    reduce_scatter x1, waiting for transfers between devices, body(): lax.psum_scatter(input_terms.astype(jnp.bfloat16), 'tensor', scatter_dime...  31.1 us
    all_gather x1, waiting for transfers between devices, body(): gathered = lax.all_gather(inputs, 'tensor', axis=1, tiled=True)  22.4 us
  transfers between devices with their start and end apart: 4, of which 3 were waited for; matrix products, arithmetic and copies ran while one was open for 7% of the time, Pallas kernels for 0%

commit v1 on v0

v1 whole, which is shorter than its diff:
```python
import jax
import jax.numpy as jnp
from jax import lax
from jax.sharding import PartitionSpec as P

surrogate_slope = 2.0
fire_level = 0.5


def unit_gradients(membrane, spike_grad, decay):
    scaled = surrogate_slope * (membrane - fire_level)
    logistic = jax.nn.sigmoid(scaled)
    surrogate = surrogate_slope * logistic * (1.0 - logistic)
    local_terms = spike_grad.astype(jnp.float32) * surrogate
    carried = jnp.zeros_like(local_terms[0])
    results = []
    for step in reversed(range(local_terms.shape[0])):
        carried = local_terms[step] + decay * carried
        results.append(carried)
    return jnp.stack(results[::-1]).astype(jnp.bfloat16)


def body(inputs, membrane, spike_grad, decay, gate_weight):
    dp_count = lax.axis_size("dp")
    tensor_count = lax.axis_size("tensor")
    steps, own, features = inputs.shape
    rows = features // dp_count
    unit_grad = unit_gradients(membrane, spike_grad, decay)
    tokens, hidden = unit_grad.shape[1:]
    units = lax.all_gather(
        unit_grad.reshape(steps * tokens, hidden), "dp", axis=0, tiled=True
    )
    columns = inputs.reshape(steps * own, dp_count, rows).transpose(1, 0, 2)
    columns = lax.all_to_all(columns, "dp", split_axis=0, concat_axis=0, tiled=True)
    columns = columns.reshape(dp_count * steps, own, rows)
    columns = lax.all_gather(columns, "tensor", axis=1, tiled=True)
    columns = columns.reshape(dp_count * steps * tokens, rows)
    partial = lax.dot_general(
        units, gate_weight, (((1,), (1,)), ((), ())), preferred_element_type=jnp.float32
    ).astype(jnp.bfloat16)
    partial = partial.reshape(dp_count * steps, tokens, rows)
    partial = lax.psum_scatter(partial, "tensor", scatter_dimension=1, tiled=True)
    partial = partial.reshape(dp_count, steps * own, rows)
    arrived = lax.all_to_all(partial, "dp", split_axis=0, concat_axis=0, tiled=True)
    input_grad = arrived.transpose(1, 0, 2).reshape(steps, own, features)
    weight_grad = lax.dot_general(
        columns, units, (((0,), (0,)), ((), ())), preferred_element_type=jnp.float32
    )
    weight_grad = (weight_grad / dp_count).astype(jnp.bfloat16)
    return (input_grad, weight_grad)


def solution(mesh):
    return jax.shard_map(
        body,
        mesh=mesh,
        in_specs=(
            P(None, ("dp", "tensor"), None),
            P(None, "dp", "tensor"),
            P(None, "dp", "tensor"),
            P("tensor"),
            P("dp", "tensor"),
        ),
        out_specs=(P(None, ("dp", "tensor"), None), P("dp", "tensor")),
        check_vma=False,
    )
```

time: 1070 us -> 313 us (0.29)
  waiting for transfers between devices: 975 us -> 235 us
  local copies, waits for them, and re-layouts: 26.1 us -> 7.58 us
  blocking collectives: 0 us -> 17.5 us
  other arithmetic: 23.2 us -> 6.51 us
    all_gather x2, waiting for transfers between devices: 942 us -> 224 us  [the longest x1 205 us: body(): lax.all_gather(unit_grad.reshape(steps * tokens, hidden), 'dp', axis=0, t...]
    reduce_scatter x1, waiting for transfers between devices: 31.1 us -> 11.9 us  [body(): lax.psum_scatter(partial, 'tensor', scatter_dimension=1, tiled=True)]
    reshape x1, local copies, waits for them, and re-layouts: 20.2 us -> 1.03 us  [body(): input_grad = arrived.transpose(1, 0, 2).reshape(steps, own, features)]
    all_to_all x0 -> x1, blocking collectives: none -> 17.5 us  [body(): lax.all_to_all(columns, 'dp', split_axis=0, concat_axis=0, tiled=True)]
    reduce_sum x1 -> x0, other arithmetic: 13.4 us -> none  [body(): total_sum = jnp.sum(arrived, axis=0, dtype=jnp.float32)]
  transfers between devices with their start and end apart: 4 -> 4, of which waited for: 3 -> 3; matrix products, arithmetic and copies ran while one was open for 7% -> 6% of each run, Pallas kernels for 0% -> 0%
where the time goes in v1:
time: 313 us
  waiting for transfers between devices  235 us (75%)
  matrix products  26 us (8%)
  blocking collectives  17.5 us (6%)
  between operations  13.8 us (4%)
  local copies, waits for them, and re-layouts  7.58 us (2%)
  other arithmetic  6.51 us (2%)
  starting transfers between devices  5.62 us (2%)
    all_gather x1, waiting for transfers between devices, body(): lax.all_gather(unit_grad.reshape(steps * tokens, hidden), 'dp', axis=0, t...  205 us
    all_gather x1, waiting for transfers between devices, body(): columns = lax.all_gather(columns, 'tensor', axis=1, tiled=True)  18.8 us
    all_to_all x1, blocking collectives, body(): lax.all_to_all(columns, 'dp', split_axis=0, concat_axis=0, tiled=True)  17.5 us
    dot_general x1, matrix products, body(): lax.dot_general(units, gate_weight, (((1,), (1,)), ((), ())), preferred_e...  13.1 us
    dot_general x1, matrix products, body(): lax.dot_general(columns, units, (((0,), (0,)), ((), ())), preferred_eleme...  13 us
    reduce_scatter x1, waiting for transfers between devices, body(): lax.psum_scatter(partial, 'tensor', scatter_dimension=1, tiled=True)  11.9 us
  transfers between devices with their start and end apart: 4, of which 3 were waited for; matrix products, arithmetic and copies ran while one was open for 6% of the time, Pallas kernels for 0%

profile of v1, /device:TPU:0, one launch (start us, length us, event | category | flops | bytes accessed | tf_op | source)
XLA Modules:
  0.0 312.5 jit_solution(7367499150260978523)
XLA Ops:
  7.2 0.0 all-gather.3.cloned.1.call-start
  7.2 0.7 broadcast_multiply_fusion
  7.9 0.0 copy-start.1
  7.9 3.9 %multiply_multiply_fusion = f32[4,64,3584]{2,1,0:T(8,128)S(1)} fusion(f32[4,64,3584]{2,1,0:T(8,128)} %param.6, bf16[4,64,3584]{2,1,0:T(8,128)(2,1)} %param.7), kind=kLoop, calls=%fused_computation.2 | loop fusion | flops 9175040 | bytes 9175040 | tf_op jit(solution)/shard_map/mul | solution.py:14
  11.9 0.0 copy-done.1
  11.9 0.3 fusion.1
  12.1 0.1 fusion.3
  12.3 1.5 pad_maximum_fusion
  13.7 0.0 all-gather.3.cloned.1.call-update
  13.8 0.0 copy-start
  13.8 0.0 reduce-scatter.2.cloned.1.call-start
  13.8 204.8 %all-gather.3.cloned.1.call-done = bf16[2048,3584]{1,0:T(8,128)(2,1)} async-done(((bf16[256,3584]{1,0:T(8,128)(2,1)}), bf16[2048,3584]{1,0:T(8,128)(2,1)}) %all-gather.3.cloned.1.call-update) | async-done | bytes 14680080 | tf_op jit(solution)/shard_map/all_gather | solution.py:30
  218.6 13.1 %convolution_convert_fusion = bf16[2048,512]{1,0:T(8,128)(2,1)} fusion(bf16[2048,3584]{1,0:T(8,128)(2,1)} %all-gather.3.cloned.1.call-done, bf16[512,3584]{1,0:T(8,128)(2,1)} %param.9), kind=kOutput, calls=%fused_computation.3 | convolution fusion | flops 7517241344 | bytes 20447232 | tf_op jit(solution)/shard_map/dot_general | solution.py:38
  231.7 0.0 reduce-scatter.2.cloned.1.call-update
  231.7 0.0 all-gather.5.cloned.1.call-start
  231.8 0.0 copy-done
  231.8 0.2 copy.19
  232.0 0.2 copy.17
  232.1 17.5 %all_to_all.10 = bf16[8,64,512]{2,1,0:T(8,128)(2,1)} all-to-all(bf16[8,64,512]{2,1,0:T(8,128)(2,1)S(1)} %copy.17), channel_id=1, replica_groups=mesh['dp'=8,'tensor'=4] {'dp'}, dimensions={0} | all-to-all | bytes 1048576 | tf_op jit(solution)/shard_map/all_to_all | solution.py:34
  249.6 0.0 all-gather.5.cloned.1.call-update
  249.6 11.9 %reduce-scatter.2.cloned.1.call-done = bf16[32,16,512]{2,1,0:T(8,128)(2,1)} async-done(((bf16[32,64,512]{2,1,0:T(8,128)(2,1)}), bf16[32,16,512]{2,1,0:T(8,128)(2,1)}) %reduce-scatter.2.cloned.1.call-update) | async-done | bytes 524304 | tf_op jit(solution)/shard_map/reduce_scatter | solution.py:42
  261.5 5.5 %all-to-all-start = ((bf16[8,64,512]{2,1,0:T(8,128)(2,1)}), bf16[8,64,512]{2,1,0:T(8,128)(2,1)S(1)}, u32[]{:S(2)}, u32[]{:S(2)}) async-start(bf16[8,64,512]{2,1,0:T(8,128)(2,1)} %bitcast.23), calls=%async_computation.1 | async-start | bytes 1048576 | tf_op jit(solution)/shard_map/all_to_all | solution.py:44
  267.0 18.8 %all-gather.5.cloned.1.call-done = bf16[32,64,512]{2,1,0:T(8,128)(2,1)} async-done(((bf16[32,16,512]{2,1,0:T(8,128)(2,1)}), bf16[32,64,512]{2,1,0:T(8,128)(2,1)}) %all-gather.5.cloned.1.call-update) | async-done | bytes 2097168 | tf_op jit(solution)/shard_map/all_gather | solution.py:36
  285.8 13.0 %fusion = bf16[512,3584]{0,1:T(8,128)(2,1)} fusion(bf16[2048,3584]{1,0:T(8,128)(2,1)} %all-gather.3.cloned.1.call-done, bf16[2048,512]{1,0:T(8,128)(2,1)} %bitcast.24), kind=kOutput, calls=%fused_computation.1 | convolution fusion | flops 7519862784 | bytes 20447232 | tf_op jit(solution)/shard_map/dot_general | solution.py:46
  298.7 5.9 %copy.18 = bf16[512,3584]{1,0:T(8,128)(2,1)} copy(bf16[512,3584]{0,1:T(8,128)(2,1)} %fusion) | data formatting | bytes 7340032
  304.6 0.0 all-to-all-done
  304.6 0.3 copy.16
  304.9 1.0 reshape.79
Async XLA Ops:
  7.2 211.5 %all-gather.3.cloned.1.call-start = ((), (), s32[]{:S(2)}) async-start(), calls=%async_computation.3 | async-start | bytes 16515072 | tf_op jit(solution)/shard_map/all_gather | solution.py:30
  7.9 3.9 %copy-start.1 = (f32[3584]{0:T(1024)S(1)}, f32[3584]{0:T(1024)}, u32[]{:S(2)}) copy-start(f32[3584]{0:T(1024)} %param.8) | copy-start | bytes 43012
  13.8 218.0 %copy-start = (bf16[4,16,4096]{2,1,0:T(8,128)(2,1)S(1)}, bf16[4,16,4096]{2,1,0:T(8,128)(2,1)}, u32[]{:S(2)}) copy-start(bf16[4,16,4096]{2,1,0:T(8,128)(2,1)} %param.5) | copy-start | bytes 1572868
  13.8 247.7 %reduce-scatter.2.cloned.1.call-start = ((), (), s32[]{:S(2)}) async-start(), calls=%async_computation.4 | async-start | bytes 2621440 | tf_op jit(solution)/shard_map/reduce_scatter | solution.py:42
  231.7 54.0 %all-gather.5.cloned.1.call-start = ((), (), s32[]{:S(2)}) async-start(), calls=%async_computation.5 | async-start | bytes 2621440 | tf_op jit(solution)/shard_map/all_gather | solution.py:36
  261.5 43.1 %all-to-all-start = ((bf16[8,64,512]{2,1,0:T(8,128)(2,1)}), bf16[8,64,512]{2,1,0:T(8,128)(2,1)S(1)}, u32[]{:S(2)}, u32[]{:S(2)}) async-start(bf16[8,64,512]{2,1,0:T(8,128)(2,1)} %bitcast.23), calls=%async_computation.1 | async-start | bytes 1048576 | tf_op jit(solution)/shard_map/all_to_all | solution.py:44
Sparse Core Ops, SparseCore 0:
  13.9 204.6 all-gather.2
  231.8 29.6 reduce-scatter.1
  263.1 22.5 all-gather.4

commit v2 on v1

v2 whole, which is shorter than its diff:
```python
import functools

import jax
import jax.numpy as jnp
from jax import lax
from jax.experimental import pallas as pl
from jax.experimental.pallas import tpu as pltpu
from jax.sharding import PartitionSpec as P

surrogate_slope = 2.0
fire_level = 0.5
MESH = pl.DeviceIdType.MESH
X = 2
TILES = 7


def unit_gradients(membrane, spike_grad, decay):
    scaled = surrogate_slope * (membrane - fire_level)
    logistic = jax.nn.sigmoid(scaled)
    surrogate = surrogate_slope * logistic * (1.0 - logistic)
    local_terms = spike_grad.astype(jnp.float32) * surrogate
    carried = jnp.zeros_like(local_terms[0])
    results = []
    for step in reversed(range(local_terms.shape[0])):
        carried = local_terms[step] + decay * carried
        results.append(carried)
    return jnp.stack(results[::-1]).astype(jnp.bfloat16)


def kernel(
    DP, T,
    inp, unit, gate, ig_out, wg_out,
    units, cols, weight, total, acc, part, arrived, reduced, grads, wide,
    loc, in1_s, in1_r, in2_s, in2_r, u_r, z_s, d_s, x_s, p_s, p_r, g_s, g_r,
):
    dp, t = lax.axis_index("dp"), lax.axis_index("tensor")
    Z = DP // X
    z, x = dp // X, dp % X
    R = gate.shape[0]
    F = gate.shape[1]
    W = F // TILES

    def remote(src, dst, ss, rs, d, tt):
        return pltpu.make_async_remote_copy(
            src_ref=src, dst_ref=dst, send_sem=ss, recv_sem=rs,
            device_id=(d, tt), device_id_type=MESH,
        )

    def wait(ref, sem):
        pltpu.make_async_copy(ref, ref, sem).wait()

    def columns(ref, d):
        return ref.at[:, pl.ds(pl.multiple_of(d * R, R), R)]

    own_w = pltpu.make_async_copy(gate, weight, loc.at[0])
    own_u = pltpu.make_async_copy(unit, units.at[dp], loc.at[1])
    own_c = pltpu.make_async_copy(columns(inp, dp), cols.at[dp, t], loc.at[2])
    own_w.start()
    own_u.start()
    own_c.start()

    barrier = pltpu.get_barrier_semaphore()

    @pl.loop(1, DP)
    def _(i):
        pl.semaphore_signal(barrier, inc=1, device_id=((dp + i) % DP, t), device_id_type=MESH)

    @pl.loop(1, T)
    def _(i):
        pl.semaphore_signal(barrier, inc=1, device_id=(dp, (t + i) % T), device_id_type=MESH)

    pl.semaphore_wait(barrier, DP + T - 2)

    def in1(d, source):
        return remote(columns(inp, d), cols.at[source, t], in1_s.at[d], in1_r.at[source], d, t)

    @pl.loop(1, DP)
    def _(i):
        in1((dp + i) % DP, dp).start()

    def up(b):
        return remote(units.at[b], units.at[b], z_s.at[b], u_r.at[b], dp + X, t)

    def down(b):
        return remote(units.at[b], units.at[b], d_s.at[b], u_r.at[b], dp - X, t)

    def cross(b):
        return remote(units.at[b], units.at[b], x_s.at[b], u_r.at[b], z * X + (1 - x), t)

    own_u.wait()

    @pl.when(z < Z - 1)
    def _():
        up(dp).start()

    @pl.when(z > 0)
    def _():
        down(dp).start()

    cross(dp).start()

    total[...] = jnp.zeros_like(total)
    own_w.wait()
    own_c.wait()

    @pl.loop(1, DP)
    def _(i):
        b = (dp + i) % DP
        wait(cols.at[b, t], in1_r.at[b])

    def in2(peer, source):
        return remote(cols.at[:, t], cols.at[:, t], in2_s.at[peer], in2_r.at[t], dp, peer)

    @pl.loop(1, T)
    def _(i):
        in2((t + i) % T, t).start()

    @pl.loop(1, T)
    def _(i):
        s = (t + i) % T
        wait(cols.at[:, s], in2_r.at[s])

    rows = unit.shape[0]
    own = rows // T

    def compute(b):
        acc[...] = jnp.zeros_like(acc)
        a = cols[b].reshape(rows, R)

        @pl.loop(0, TILES)
        def _(j):
            tile = pl.ds(pl.multiple_of(j * W, W), W)
            u = units[b, :, tile]
            acc[...] += lax.dot_general(
                u, weight[:, tile], (((1,), (1,)), ((), ())), preferred_element_type=jnp.float32
            )
            total[:, tile] += lax.dot_general(
                a, u, (((0,), (0,)), ((), ())), preferred_element_type=jnp.float32
            )

        part[b] = acc[...].astype(jnp.bfloat16).reshape(T, own, R)

        @pl.loop(1, T)
        def _(i):
            peer = (t + i) % T
            remote(part.at[b, peer], arrived.at[b, i - 1], p_s.at[b], p_r.at[b], dp, peer).start()

    def reduce(b):
        wait(arrived.at[b], p_r.at[b])
        value = part[b, t].astype(jnp.float32)
        for i in range(T - 1):
            value += arrived[b, i].astype(jnp.float32)
        reduced[b] = value.astype(jnp.bfloat16)

        @pl.when(b != dp)
        def _():
            remote(reduced.at[b], columns(grads, dp), g_s.at[b], g_r.at[dp], b, t).start()

        @pl.when(b == dp)
        def _():
            pltpu.make_async_copy(reduced.at[b], columns(grads, dp), g_s.at[b]).start()

    def sides(k, do, column):
        @pl.when((k >= 0) & (k < Z) & (z - k >= 0))
        def _():
            do((z - k) * X + column)

        @pl.when((k > 0) & (z + k < Z))
        def _():
            do((z + k) * X + column)

    def take(b):
        @pl.when(b != dp)
        def _():
            wait(units.at[b], u_r.at[b])

            @pl.when((b < dp) & (z < Z - 1))
            def _():
                up(b).start()

            @pl.when((b > dp) & (z > 0))
            def _():
                down(b).start()

            cross(b).start()

    def take_across(b):
        wait(units.at[b], u_r.at[b])
        compute(b)

    @pl.loop(0, Z + 2)
    def _(k):
        sides(k, take, x)
        sides(k, compute, x)
        sides(k - 1, take_across, 1 - x)
        sides(k - 1, reduce, x)
        sides(k - 2, reduce, 1 - x)

    out_tiles = TILES

    @pl.loop(0, out_tiles)
    def _(j):
        tile = pl.ds(pl.multiple_of(j * W, W), W)
        wide[:, tile] = (total[:, tile] / DP).astype(jnp.bfloat16)

    out_w = pltpu.make_async_copy(wide, wg_out, loc.at[0])
    out_w.start()

    @pl.loop(0, DP)
    def _(b):
        @pl.when(b != dp)
        def _():
            wait(columns(grads, b), g_r.at[b])

        wait(reduced.at[b], g_s.at[b])
        wait(arrived.at[b], p_s.at[b])

    out_i = pltpu.make_async_copy(grads, ig_out, loc.at[1])
    out_i.start()

    @pl.loop(1, DP)
    def _(i):
        wait(cols.at[0, 0], in1_s.at[(dp + i) % DP])

    @pl.loop(1, T)
    def _(i):
        wait(cols.at[:, 0], in2_s.at[(t + i) % T])

    @pl.loop(0, Z)
    def _(c):
        b = c * X + x
        wait(units.at[b], x_s.at[b])

        @pl.when((c <= z) & (z < Z - 1))
        def _():
            wait(units.at[b], z_s.at[b])

        @pl.when((c >= z) & (z > 0))
        def _():
            wait(units.at[b], d_s.at[b])

    out_w.wait()
    out_i.wait()


def body(inputs, membrane, spike_grad, decay, gate_weight):
    DP, T = lax.axis_size("dp"), lax.axis_size("tensor")
    steps, own, features = inputs.shape
    R, F = gate_weight.shape
    unit_grad = unit_gradients(membrane, spike_grad, decay)
    rows = steps * own * T
    unit = unit_grad.reshape(steps, T, own, F).transpose(1, 0, 2, 3).reshape(rows, F)
    inp = inputs.reshape(steps * own, features)
    bf, f32 = jnp.bfloat16, jnp.float32
    dma = pltpu.SemaphoreType.DMA
    ig, wg = pl.pallas_call(
        functools.partial(kernel, DP, T),
        out_shape=(
            jax.ShapeDtypeStruct((steps * own, features), bf),
            jax.ShapeDtypeStruct((R, F), bf),
        ),
        in_specs=[pl.BlockSpec(memory_space=pl.ANY)] * 3,
        out_specs=(pl.BlockSpec(memory_space=pl.ANY),) * 2,
        scratch_shapes=[
            pltpu.VMEM((DP, rows, F), bf),
            pltpu.VMEM((DP, T, rows // T, R), bf),
            pltpu.VMEM((R, F), bf),
            pltpu.VMEM((R, F), f32),
            pltpu.VMEM((rows, R), f32),
            pltpu.VMEM((DP, T, rows // T, R), bf),
            pltpu.VMEM((DP, T - 1, rows // T, R), bf),
            pltpu.VMEM((DP, rows // T, R), bf),
            pltpu.VMEM((steps * own, features), bf),
            pltpu.VMEM((R, F), bf),
            dma((3,)), dma((DP,)), dma((DP,)), dma((T,)), dma((T,)),
            dma((DP,)), dma((DP,)), dma((DP,)), dma((DP,)),
            dma((DP,)), dma((DP,)), dma((DP,)), dma((DP,)),
        ],
        compiler_params=pltpu.CompilerParams(
            collective_id=0, has_side_effects=True, vmem_limit_bytes=56 * 1024 * 1024
        ),
        cost_estimate=pl.CostEstimate(
            flops=4 * DP * rows * R * F, bytes_accessed=4 * R * F + 2 * rows * F, transcendentals=0
        ),
    )(inp, unit, gate_weight)
    return (ig.reshape(steps, own, features), wg)


def solution(mesh):
    return jax.shard_map(
        body,
        mesh=mesh,
        in_specs=(
            P(None, ("dp", "tensor"), None),
            P(None, "dp", "tensor"),
            P(None, "dp", "tensor"),
            P("tensor"),
            P("dp", "tensor"),
        ),
        out_specs=(P(None, ("dp", "tensor"), None), P("dp", "tensor")),
        check_vma=False,
    )
```

time: 313 us -> 206 us (0.66)
  waiting for transfers between devices: 235 us -> 0 us
  Pallas kernels: 0 us -> 192 us
  matrix products: 26 us -> 0 us
  blocking collectives: 17.5 us -> 0 us
  between operations: 13.8 us -> 0.66 us
  starting transfers between devices: 5.62 us -> 0 us
    all_gather x2 -> x0, waiting for transfers between devices: 224 us -> none  [the longest x1 205 us: body(): lax.all_gather(unit_grad.reshape(steps * tokens, hidden), 'dp', axis=0, t...]
    pallas_call x0 -> x1, Pallas kernels: none -> 192 us  [body(): pl.pallas_call(functools.partial(kernel, DP, T), out_shape=(jax.ShapeDtyp...]
    dot_general x2 -> x0, matrix products: 26 us -> none  [the longest x1 13.1 us: body(): lax.dot_general(units, gate_weight, (((1,), (1,)), ((), ())), preferred_e...]
    all_to_all x1 -> x0, blocking collectives: 17.5 us -> none  [body(): lax.all_to_all(columns, 'dp', split_axis=0, concat_axis=0, tiled=True)]
    reduce_scatter x1 -> x0, waiting for transfers between devices: 11.9 us -> none  [body(): lax.psum_scatter(partial, 'tensor', scatter_dimension=1, tiled=True)]
    all_to_all x1 -> x0, starting transfers between devices: 5.5 us -> none  [body(): lax.all_to_all(partial, 'dp', split_axis=0, concat_axis=0, tiled=True)]
  transfers between devices with their start and end apart: 4 -> 0, of which waited for: 3 -> 0; matrix products, arithmetic and copies ran while one was open for 6% -> 0% of each run, Pallas kernels for 0% -> 0%
where the time goes in v2:
time: 206 us
  Pallas kernels  192 us (93%)
  other arithmetic  6.51 us (3%)
  local copies, waits for them, and re-layouts  5.98 us (3%)
    pallas_call x1, Pallas kernels, body(): pl.pallas_call(functools.partial(kernel, DP, T), out_shape=(jax.ShapeDtyp...  192 us
    unnamed x4, local copies, waits for them, and re-layouts  5.98 us

profile of v2, /device:TPU:0, one launch (start us, length us, event | category | flops | bytes accessed | tf_op | source)
XLA Modules:
  0.0 205.6 jit_solution(5797434818229150013)
XLA Ops:
  0.6 0.7 broadcast_multiply_fusion
  1.4 0.0 copy-start
  1.4 3.9 %multiply_multiply_fusion = f32[4,64,3584]{2,1,0:T(8,128)S(1)} fusion(f32[4,64,3584]{2,1,0:T(8,128)} %param.6, bf16[4,64,3584]{2,1,0:T(8,128)(2,1)} %param.7), kind=kLoop, calls=%fused_computation | loop fusion | flops 9175040 | bytes 9175040 | tf_op jit(solution)/shard_map/mul | solution.py:21
  5.3 0.0 copy-done
  5.3 0.3 fusion
  5.6 0.1 fusion.2
  5.7 1.5 pad_maximum_fusion
  7.2 192.5 %shard_map.68 = (bf16[64,4096]{1,0:T(8,128)(2,1)}, bf16[512,3584]{1,0:T(8,128)(2,1)}) custom-call(bf16[64,4096]{1,0:T(8,128)(2,1)} %bitcast.23, bf16[256,3584]{1,0:T(8,128)(2,1)} %bitcast.17, bf16[512,3584]{1,0:T(8,128)(2,1)} %gate.1), custom_call_target="tpu_custom_call" | custom-call | flops 15032385536 | bytes 9175040 | tf_op jit(solution)/shard_map/pallas_call | solution.py:256
  199.7 1.9 copy.13
  201.5 4.1 %copy.14 = bf16[512,3584]{1,0:T(8,128)(2,1)} copy(bf16[512,3584]{1,0:T(8,128)(2,1)} %get-tuple-element.14) | data formatting | bytes 7340032
Async XLA Ops:
  1.4 3.9 %copy-start = (f32[3584]{0:T(1024)S(1)}, f32[3584]{0:T(1024)}, u32[]{:S(2)}) copy-start(f32[3584]{0:T(1024)} %param.8) | copy-start | bytes 43012

commit v3 on v2

--- a/solution.py
+++ b/solution.py
@@ -31,7 +31,7 @@
     DP, T,
     inp, unit, gate, ig_out, wg_out,
     units, cols, weight, total, acc, part, arrived, reduced, grads, wide,
-    loc, in1_s, in1_r, in2_s, in2_r, u_r, z_s, d_s, x_s, p_s, p_r, g_s, g_r,
+    loc, in1_s, in1_r, in2_s, in2_r, u_r, v_r, z_s, d_s, b_s, x_s, p_s, p_r, g_s, g_r,
 ):
     dp, t = lax.axis_index("dp"), lax.axis_index("tensor")
     Z = DP // X
@@ -78,26 +78,50 @@
     def _(i):
         in1((dp + i) % DP, dp).start()
 
-    def up(b):
-        return remote(units.at[b], units.at[b], z_s.at[b], u_r.at[b], dp + X, t)
-
-    def down(b):
-        return remote(units.at[b], units.at[b], d_s.at[b], u_r.at[b], dp - X, t)
-
-    def cross(b):
-        return remote(units.at[b], units.at[b], x_s.at[b], u_r.at[b], z * X + (1 - x), t)
+    rows = unit.shape[0]
+    own = rows // T
+    half = rows // 2
+
+    def whole(b):
+        return units.at[b]
+
+    def first(b):
+        return units.at[b, pl.ds(0, half)]
+
+    def second(b):
+        return units.at[b, pl.ds(half, half)]
+
+    def up(ref, b, ss=z_s, rs=u_r):
+        remote(ref, ref, ss.at[b], rs.at[b], dp + X, t).start()
+
+    def down(ref, b, ss=d_s, rs=u_r):
+        remote(ref, ref, ss.at[b], rs.at[b], dp - X, t).start()
+
+    def cross(ref, b):
+        remote(ref, ref, x_s.at[b], u_r.at[b], z * X + (1 - x), t).start()
+
+    def is_end(b):
+        return (b < X) | (b >= DP - X)
 
     own_u.wait()
 
-    @pl.when(z < Z - 1)
+    @pl.when(z == 0)
     def _():
-        up(dp).start()
-
-    @pl.when(z > 0)
+        up(first(dp), dp)
+        cross(whole(dp), dp)
+        up(second(dp), dp, b_s, v_r)
+
+    @pl.when(z == Z - 1)
     def _():
-        down(dp).start()
-
-    cross(dp).start()
+        down(first(dp), dp)
+        cross(whole(dp), dp)
+        down(second(dp), dp, b_s, v_r)
+
+    @pl.when((z > 0) & (z < Z - 1))
+    def _():
+        up(whole(dp), dp)
+        down(whole(dp), dp)
+        cross(whole(dp), dp)
 
     total[...] = jnp.zeros_like(total)
     own_w.wait()
@@ -119,9 +143,6 @@
     def _(i):
         s = (t + i) % T
         wait(cols.at[:, s], in2_r.at[s])
-
-    rows = unit.shape[0]
-    own = rows // T
 
     def compute(b):
         acc[...] = jnp.zeros_like(acc)
@@ -169,30 +190,81 @@
         def _():
             do((z + k) * X + column)
 
+    def forward(ref, b, up_s=z_s, down_s=d_s, rs=u_r):
+        @pl.when((b < z * X) & (z < Z - 1))
+        def _():
+            up(ref, b, up_s, rs)
+
+        @pl.when((b >= (z + 1) * X) & (z > 0))
+        def _():
+            down(ref, b, down_s, rs)
+
     def take(b):
-        @pl.when(b != dp)
-        def _():
-            wait(units.at[b], u_r.at[b])
-
-            @pl.when((b < dp) & (z < Z - 1))
+        @pl.when((b != dp) & is_end(b))
+        def _():
+            wait(first(b), u_r.at[b])
+            forward(first(b), b)
+            cross(first(b), b)
+
+        @pl.when((b != dp) & jnp.logical_not(is_end(b)))
+        def _():
+            wait(whole(b), u_r.at[b])
+            forward(whole(b), b)
+            cross(whole(b), b)
+
+    def is_split(b):
+        return is_end(b) & (b // X != z)
+
+    def compute_whole(b):
+        @pl.when(jnp.logical_not(is_split(b)))
+        def _():
+            compute(b)
+
+    def across_whole(b):
+        @pl.when(jnp.logical_not(is_split(b)))
+        def _():
+            wait(whole(b), u_r.at[b])
+
+            @pl.when(z == 0)
             def _():
-                up(b).start()
-
-            @pl.when((b > dp) & (z > 0))
+                @pl.when(b < X)
+                def _():
+                    up(second(b), b, b_s, v_r)
+
+            @pl.when(z == Z - 1)
             def _():
-                down(b).start()
-
-            cross(b).start()
-
-    def take_across(b):
-        wait(units.at[b], u_r.at[b])
-        compute(b)
+                @pl.when(b >= DP - X)
+                def _():
+                    down(second(b), b, b_s, v_r)
+
+            compute(b)
+
+    def take_second(b):
+        @pl.when(is_split(b))
+        def _():
+            wait(second(b), v_r.at[b])
+            forward(second(b), b, b_s, b_s, v_r)
+
+    def compute_split(b):
+        @pl.when(is_split(b))
+        def _():
+            compute(b)
+
+    def across_split(b):
+        @pl.when(is_split(b))
+        def _():
+            wait(first(b), u_r.at[b])
+            compute(b)
 
     @pl.loop(0, Z + 2)
     def _(k):
         sides(k, take, x)
-        sides(k, compute, x)
-        sides(k - 1, take_across, 1 - x)
+        sides(k, compute_whole, x)
+        sides(k - 1, across_whole, 1 - x)
+        sides(k, take_second, x)
+        sides(k, take_second, 1 - x)
+        sides(k, compute_split, x)
+        sides(k - 1, across_split, 1 - x)
         sides(k - 1, reduce, x)
         sides(k - 2, reduce, 1 - x)
 
@@ -226,18 +298,31 @@
     def _(i):
         wait(cols.at[:, 0], in2_s.at[(t + i) % T])
 
+    def sent(b, cond, sem, split):
+        @pl.when(cond & split)
+        def _():
+            wait(first(b), sem.at[b])
+
+        @pl.when(cond & jnp.logical_not(split))
+        def _():
+            wait(whole(b), sem.at[b])
+
     @pl.loop(0, Z)
     def _(c):
         b = c * X + x
-        wait(units.at[b], x_s.at[b])
-
-        @pl.when((c <= z) & (z < Z - 1))
-        def _():
-            wait(units.at[b], z_s.at[b])
-
-        @pl.when((c >= z) & (z > 0))
-        def _():
-            wait(units.at[b], d_s.at[b])
+        sent(b, c >= 0, x_s, is_split(b))
+        sent(b, (c <= z) & (z < Z - 1), z_s, is_end(b))
+        sent(b, (c >= z) & (z > 0), d_s, is_end(b))
+
+    @pl.loop(0, X)
+    def _(c):
+        @pl.when(z < Z - 1)
+        def _():
+            wait(second(c), b_s.at[c])
+
+        @pl.when(z > 0)
+        def _():
+            wait(second(DP - X + c), b_s.at[DP - X + c])
 
     out_w.wait()
     out_i.wait()
@@ -273,7 +358,7 @@
             pltpu.VMEM((steps * own, features), bf),
             pltpu.VMEM((R, F), bf),
             dma((3,)), dma((DP,)), dma((DP,)), dma((T,)), dma((T,)),
-            dma((DP,)), dma((DP,)), dma((DP,)), dma((DP,)),
+            dma((DP,)), dma((DP,)), dma((DP,)), dma((DP,)), dma((DP,)), dma((DP,)),
             dma((DP,)), dma((DP,)), dma((DP,)), dma((DP,)),
         ],
         compiler_params=pltpu.CompilerParams(

time: 206 us -> 192 us (0.932)
  Pallas kernels: 192 us -> 179 us
    pallas_call x1, Pallas kernels: 192 us -> 179 us  [body(): pl.pallas_call(functools.partial(kernel, DP, T), out_shape=(jax.ShapeDtyp...]
where the time goes in v3:
time: 192 us
  Pallas kernels  179 us (93%)
  other arithmetic  6.51 us (3%)
  local copies, waits for them, and re-layouts  5.98 us (3%)
    pallas_call x1, Pallas kernels, body(): pl.pallas_call(functools.partial(kernel, DP, T), out_shape=(jax.ShapeDtyp...  179 us
    unnamed x4, local copies, waits for them, and re-layouts  5.98 us
    mul x1, other arithmetic, unit_gradients(): local_terms = spike_grad.astype(jnp.float32) * surrogate  3.93 us

profile of v3, /device:TPU:0, one launch (start us, length us, event | category | flops | bytes accessed | tf_op | source)
XLA Modules:
  0.0 191.7 jit_solution(15413593016775064783)
XLA Ops:
  0.6 0.7 broadcast_multiply_fusion
  1.4 0.0 copy-start
  1.4 3.9 %multiply_multiply_fusion = f32[4,64,3584]{2,1,0:T(8,128)S(1)} fusion(f32[4,64,3584]{2,1,0:T(8,128)} %param.6, bf16[4,64,3584]{2,1,0:T(8,128)(2,1)} %param.7), kind=kLoop, calls=%fused_computation | loop fusion | flops 9175040 | bytes 9175040 | tf_op jit(solution)/shard_map/mul | solution.py:21
  5.3 0.0 copy-done
  5.3 0.3 fusion
  5.6 0.1 fusion.2
  5.7 1.5 pad_maximum_fusion
  7.2 178.6 %shard_map.68 = (bf16[64,4096]{1,0:T(8,128)(2,1)}, bf16[512,3584]{1,0:T(8,128)(2,1)}) custom-call(bf16[64,4096]{1,0:T(8,128)(2,1)} %bitcast.23, bf16[256,3584]{1,0:T(8,128)(2,1)} %bitcast.17, bf16[512,3584]{1,0:T(8,128)(2,1)} %gate.1), custom_call_target="tpu_custom_call" | custom-call | flops 15032385536 | bytes 9175040 | tf_op jit(solution)/shard_map/pallas_call | solution.py:341
  185.8 1.9 copy.13
  187.6 4.1 %copy.14 = bf16[512,3584]{1,0:T(8,128)(2,1)} copy(bf16[512,3584]{1,0:T(8,128)(2,1)} %get-tuple-element.14) | data formatting | bytes 7340032
Async XLA Ops:
  1.4 3.9 %copy-start = (f32[3584]{0:T(1024)S(1)}, f32[3584]{0:T(1024)}, u32[]{:S(2)}) copy-start(f32[3584]{0:T(1024)} %param.8) | copy-start | bytes 43012

commit v4 on v3

--- a/solution.py
+++ b/solution.py
@@ -109,13 +109,11 @@
     def _():
         up(first(dp), dp)
         cross(whole(dp), dp)
-        up(second(dp), dp, b_s, v_r)
 
     @pl.when(z == Z - 1)
     def _():
         down(first(dp), dp)
         cross(whole(dp), dp)
-        down(second(dp), dp, b_s, v_r)
 
     @pl.when((z > 0) & (z < Z - 1))
     def _():
@@ -220,24 +218,39 @@
         def _():
             compute(b)
 
+    def across_first(b):
+        wait(whole(b), u_r.at[b])
+
+        @pl.when(z == 0)
+        def _():
+            up(second(b), b, b_s, v_r)
+
+        @pl.when(z == Z - 1)
+        def _():
+            down(second(b), b, b_s, v_r)
+
     def across_whole(b):
         @pl.when(jnp.logical_not(is_split(b)))
         def _():
-            wait(whole(b), u_r.at[b])
-
-            @pl.when(z == 0)
+            @pl.when(b // X != z)
             def _():
-                @pl.when(b < X)
-                def _():
-                    up(second(b), b, b_s, v_r)
-
-            @pl.when(z == Z - 1)
+                wait(whole(b), u_r.at[b])
+
+            compute(b)
+
+    def at_last(do):
+        def run(b):
+            @pl.when((z == 0) | (z == Z - 1))
             def _():
-                @pl.when(b >= DP - X)
-                def _():
-                    down(second(b), b, b_s, v_r)
-
-            compute(b)
+                do(b)
+        return run
+
+    def before_last(do):
+        def run(b):
+            @pl.when((z > 0) & (z < Z - 1))
+            def _():
+                do(b)
+        return run
 
     def take_second(b):
         @pl.when(is_split(b))
@@ -259,11 +272,28 @@
     @pl.loop(0, Z + 2)
     def _(k):
         sides(k, take, x)
+
+        @pl.when(k == 1)
+        def _():
+            across_first(z * X + (1 - x))
+
         sides(k, compute_whole, x)
+
+        @pl.when((k == 0) & (z == 0))
+        def _():
+            wait(first(dp), z_s.at[dp])
+            up(second(dp), dp, b_s, v_r)
+
+        @pl.when((k == 0) & (z == Z - 1))
+        def _():
+            wait(first(dp), d_s.at[dp])
+            down(second(dp), dp, b_s, v_r)
+
         sides(k - 1, across_whole, 1 - x)
         sides(k, take_second, x)
+        sides(k, at_last(compute_split), x)
         sides(k, take_second, 1 - x)
-        sides(k, compute_split, x)
+        sides(k, before_last(compute_split), x)
         sides(k - 1, across_split, 1 - x)
         sides(k - 1, reduce, x)
         sides(k - 2, reduce, 1 - x)
@@ -311,8 +341,8 @@
     def _(c):
         b = c * X + x
         sent(b, c >= 0, x_s, is_split(b))
-        sent(b, (c <= z) & (z < Z - 1), z_s, is_end(b))
-        sent(b, (c >= z) & (z > 0), d_s, is_end(b))
+        sent(b, (c <= z) & (z < Z - 1) & (z + c > 0), z_s, is_end(b))
+        sent(b, (c >= z) & (z > 0) & (z + c < 2 * Z - 2), d_s, is_end(b))
 
     @pl.loop(0, X)
     def _(c):

time: 192 us -> 189 us (0.984)
  Pallas kernels: 179 us -> 175 us
    pallas_call x1, Pallas kernels: 179 us -> 175 us  [body(): pl.pallas_call(functools.partial(kernel, DP, T), out_shape=(jax.ShapeDtyp...]
where the time goes in v4:
time: 189 us; the launch traced here: 188 us
  Pallas kernels  175 us (93%)
  other arithmetic  6.51 us (3%)
  local copies, waits for them, and re-layouts  5.98 us (3%)
    pallas_call x1, Pallas kernels, body(): pl.pallas_call(functools.partial(kernel, DP, T), out_shape=(jax.ShapeDtyp...  175 us
    unnamed x4, local copies, waits for them, and re-layouts  5.98 us
    mul x1, other arithmetic, unit_gradients(): local_terms = spike_grad.astype(jnp.float32) * surrogate  3.93 us

profile of v4, /device:TPU:0, one launch (start us, length us, event | category | flops | bytes accessed | tf_op | source)
XLA Modules:
  0.0 188.3 jit_solution(1344303053086076175)
XLA Ops:
  0.6 0.7 broadcast_multiply_fusion
  1.4 0.0 copy-start
  1.4 3.9 %multiply_multiply_fusion = f32[4,64,3584]{2,1,0:T(8,128)S(1)} fusion(f32[4,64,3584]{2,1,0:T(8,128)} %param.6, bf16[4,64,3584]{2,1,0:T(8,128)(2,1)} %param.7), kind=kLoop, calls=%fused_computation | loop fusion | flops 9175040 | bytes 9175040 | tf_op jit(solution)/shard_map/mul | solution.py:21
  5.3 0.0 copy-done
  5.3 0.3 fusion
  5.6 0.1 fusion.2
  5.7 1.5 pad_maximum_fusion
  7.2 175.2 %shard_map.68 = (bf16[64,4096]{1,0:T(8,128)(2,1)}, bf16[512,3584]{1,0:T(8,128)(2,1)}) custom-call(bf16[64,4096]{1,0:T(8,128)(2,1)} %bitcast.23, bf16[256,3584]{1,0:T(8,128)(2,1)} %bitcast.17, bf16[512,3584]{1,0:T(8,128)(2,1)} %gate.1), custom_call_target="tpu_custom_call" | custom-call | flops 15032385536 | bytes 9175040 | tf_op jit(solution)/shard_map/pallas_call | solution.py:371
  182.3 1.9 copy.13
  184.2 4.1 %copy.14 = bf16[512,3584]{1,0:T(8,128)(2,1)} copy(bf16[512,3584]{1,0:T(8,128)(2,1)} %get-tuple-element.14) | data formatting | bytes 7340032
Async XLA Ops:
  1.4 3.9 %copy-start = (f32[3584]{0:T(1024)S(1)}, f32[3584]{0:T(1024)}, u32[]{:S(2)}) copy-start(f32[3584]{0:T(1024)} %param.8) | copy-start | bytes 43012

commit v5 on v4

--- a/solution.py
+++ b/solution.py
@@ -153,9 +153,6 @@
             acc[...] += lax.dot_general(
                 u, weight[:, tile], (((1,), (1,)), ((), ())), preferred_element_type=jnp.float32
             )
-            total[:, tile] += lax.dot_general(
-                a, u, (((0,), (0,)), ((), ())), preferred_element_type=jnp.float32
-            )
 
         part[b] = acc[...].astype(jnp.bfloat16).reshape(T, own, R)
 
@@ -163,6 +160,13 @@
         def _(i):
             peer = (t + i) % T
             remote(part.at[b, peer], arrived.at[b, i - 1], p_s.at[b], p_r.at[b], dp, peer).start()
+
+        @pl.loop(0, TILES)
+        def _(j):
+            tile = pl.ds(pl.multiple_of(j * W, W), W)
+            total[:, tile] += lax.dot_general(
+                a, units[b, :, tile], (((0,), (0,)), ((), ())), preferred_element_type=jnp.float32
+            )
 
     def reduce(b):
         wait(arrived.at[b], p_r.at[b])

time: 189 us -> 188 us (level)
  no operation moved by 1% of the time
where the time goes in v5:
time: 188 us; the launch traced here: 187 us
  Pallas kernels  174 us (93%)
  other arithmetic  6.51 us (3%)
  local copies, waits for them, and re-layouts  5.98 us (3%)
    pallas_call x1, Pallas kernels, body(): pl.pallas_call(functools.partial(kernel, DP, T), out_shape=(jax.ShapeDtyp...  174 us
    unnamed x4, local copies, waits for them, and re-layouts  5.98 us
    mul x1, other arithmetic, unit_gradients(): local_terms = spike_grad.astype(jnp.float32) * surrogate  3.93 us

profile of v5, /device:TPU:0, one launch (start us, length us, event | category | flops | bytes accessed | tf_op | source)
XLA Modules:
  0.0 187.4 jit_solution(3425342969882229534)
XLA Ops:
  0.6 0.7 broadcast_multiply_fusion
  1.4 0.0 copy-start
  1.4 3.9 %multiply_multiply_fusion = f32[4,64,3584]{2,1,0:T(8,128)S(1)} fusion(f32[4,64,3584]{2,1,0:T(8,128)} %param.6, bf16[4,64,3584]{2,1,0:T(8,128)(2,1)} %param.7), kind=kLoop, calls=%fused_computation | loop fusion | flops 9175040 | bytes 9175040 | tf_op jit(solution)/shard_map/mul | solution.py:21
  5.3 0.0 copy-done
  5.3 0.3 fusion
  5.6 0.1 fusion.2
  5.7 1.5 pad_maximum_fusion
  7.2 174.2 %shard_map.68 = (bf16[64,4096]{1,0:T(8,128)(2,1)}, bf16[512,3584]{1,0:T(8,128)(2,1)}) custom-call(bf16[64,4096]{1,0:T(8,128)(2,1)} %bitcast.23, bf16[256,3584]{1,0:T(8,128)(2,1)} %bitcast.17, bf16[512,3584]{1,0:T(8,128)(2,1)} %gate.1), custom_call_target="tpu_custom_call" | custom-call | flops 15032385536 | bytes 9175040 | tf_op jit(solution)/shard_map/pallas_call | solution.py:375
  181.4 1.9 copy.13
  183.3 4.1 %copy.14 = bf16[512,3584]{1,0:T(8,128)(2,1)} copy(bf16[512,3584]{1,0:T(8,128)(2,1)} %get-tuple-element.14) | data formatting | bytes 7340032
Async XLA Ops:
  1.4 3.9 %copy-start = (f32[3584]{0:T(1024)S(1)}, f32[3584]{0:T(1024)}, u32[]{:S(2)}) copy-start(f32[3584]{0:T(1024)} %param.8) | copy-start | bytes 43012
